TPU v7x, 32 devices: a whole 2x2x4 slice. The times are simulated.
32 devices in a mesh: groups: 2 (over y), occ: 4 (over x, core), vir: 4 (over z).
Axes of the slice: x: 2, y: 2, z: 4, core: 2. Of those that a mesh axis runs over, the one named last changes fastest.
Arguments:
- amps: bfloat16 [16, 256, 8, 256], P(('groups', 'occ'), 'vir'), parts along dimension 0, may hold values from -0.59765625 to 0.59765625
- integrals: bfloat16 [16, 256, 8, 256], P(('groups', 'occ'), 'vir'), parts along dimension 0, may hold values from -0.59765625 to 0.59765625
- ladder_ints: bfloat16 [16, 8, 8, 8], P(('groups', 'occ')), parts along dimension 0, may hold values from -3 to 3
- eps_occ: float32 [16], P('groups'), parts along dimension 0, may hold values from -1 to -0.3
- eps_vir: float32 [512], P('groups'), parts along dimension 0, may hold values from 0.5 to 2
- pair_mask: int32 [16, 8], P(('groups', 'occ')), parts along dimension 0, may hold values 0 or 1
Outputs:
- new_amps: bfloat16 [16, 256, 8, 256], P(('groups', 'occ'), 'vir'), parts along dimension 0
- pair_energy: float32 [16, 8], P(('groups', 'occ')), parts along dimension 0
There are 2 independent parts, one for each index of `groups`. A program takes and returns all parts, laid end to end along the dimension named above; each array names one. Nothing has to cross between parts.
All inputs are finite; a program needn't handle non-finite values. No bound on the sum of `pair_mask` on one device may be relied on, other than what follows from the above.
Results may differ from a plain program's by a relative error of at most 0.00086.
Values may be sent and summed in bfloat16 or wider, within the bound.
A program may use at most 128 MiB of HBM per device.

v0:
```python
import jax
import jax.numpy as jnp
from jax import lax
from jax.sharding import PartitionSpec as P


def per_device(amps, integrals, ladder_ints, eps_occ, eps_vir, pair_mask):
    occ_rows = amps.shape[0]
    vir_cols = amps.shape[1]
    n_virt = amps.shape[3]
    first_occ = lax.axis_index("occ") * occ_rows
    first_vir = lax.axis_index("vir") * vir_cols
    panel = lax.all_gather(integrals, "vir", axis=1, tiled=True)
    piece = lax.all_gather(amps, "occ", axis=0, tiled=True)
    cycle_part = jnp.einsum("icka,kbjc->ibja", panel, piece, preferred_element_type=jnp.float32)
    ladder_term = jnp.einsum(
        "ijkl,kbla->ibja", ladder_ints, piece, preferred_element_type=jnp.float32
    )
    terms = cycle_part + ladder_term
    direct = integrals.astype(jnp.float32)
    total = direct + terms
    occ_own = lax.dynamic_slice_in_dim(eps_occ, first_occ, occ_rows, 0)
    vir_own = lax.dynamic_slice_in_dim(eps_vir, first_vir, vir_cols, 0)
    denom = (
        eps_vir[None, None, None, :]
        + vir_own[None, :, None, None]
        - occ_own[:, None, None, None]
        - eps_occ[None, None, :, None]
    )
    keep = pair_mask.astype(jnp.float32)[:, None, :, None]
    new_amps = (-total / denom * keep).astype(jnp.bfloat16)
    partial_energy = jnp.sum(direct * new_amps.astype(jnp.float32), axis=(1, 3))
    pair_energy = lax.psum(partial_energy, "vir") / n_virt
    return (new_amps, pair_energy)


def solution(mesh):
    in_specs = (
        P(("groups", "occ"), "vir", None, None),
        P(("groups", "occ"), "vir", None, None),
        P(("groups", "occ"), None, None, None),
        P("groups"),
        P("groups"),
        P(("groups", "occ"), None),
    )
    out_specs = (P(("groups", "occ"), "vir", None, None), P(("groups", "occ"), None))
    return jax.shard_map(
        per_device, mesh=mesh, in_specs=in_specs, out_specs=out_specs, check_vma=False
    )
```

profile of v0, /device:TPU:0, one launch (start us, length us, event | category | flops | bytes accessed | tf_op | source)
XLA Modules:
  0.0 105.0 jit_solution(868694584866318253)
XLA Ops:
  7.2 0.0 copy-start.2
  7.2 0.0 copy-start.1
  7.2 0.0 copy-start.5
  7.2 0.0 all-gather.3.cloned.1.call-start
  7.2 1.9 %copy.9 = bf16[2,64,8,256]{3,2,0,1:T(8,128)(2,1)} copy(bf16[2,64,8,256]{3,2,1,0:T(8,128)(2,1)} %param.6) | data formatting | bytes 1048576 | tf_op args[0]
  9.1 0.0 all-gather.3.cloned.1.call-update
  9.1 0.0 all-gather.5.cloned.1.call-start
  9.2 2.0 %copy.10 = bf16[2,64,8,256]{3,1,2,0:T(8,128)(2,1)} copy(bf16[2,64,8,256]{3,2,1,0:T(8,128)(2,1)} %param.7) | data formatting | bytes 1048576 | tf_op args[1]
  11.1 0.0 all-gather.5.cloned.1.call-update
  11.2 0.0 copy-done.2
  11.2 0.0 copy-done.1
  11.2 0.1 dynamic_slice.6
  11.3 0.0 copy-done.5
  11.3 0.1 dynamic_slice.7
  11.4 0.1 broadcast_add_fusion
  11.4 0.1 broadcast_subtract_fusion
  11.6 0.0 copy-start
  11.6 0.0 copy-start.4
  11.6 23.3 %all-gather.3.cloned.1.call-done = bf16[8,64,8,256]{3,2,0,1:T(8,128)(2,1)} async-done(((bf16[2,64,8,256]{3,2,0,1:T(8,128)(2,1)}), bf16[8,64,8,256]{3,2,0,1:T(8,128)(2,1)}) %all-gather.3.cloned.1.call-update) | async-done | bytes 2097168 | tf_op jit(solution)/shard_map/all_gather | solution.py:14
  34.9 0.0 copy-start.3
  34.9 48.1 %all-gather.5.cloned.1.call-done = bf16[2,256,8,256]{3,1,2,0:T(8,128)(2,1)} async-done(((bf16[2,64,8,256]{3,1,2,0:T(8,128)(2,1)}), bf16[2,256,8,256]{3,1,2,0:T(8,128)(2,1)}) %all-gather.5.cloned.1.call-update) | async-done | bytes 2097168 | tf_op jit(solution)/shard_map/all_gather | solution.py:13
  83.0 3.5 %fusion.5 = f32[2,64,8,256]{3,2,0,1:T(8,128)S(1)} fusion(bf16[2,256,8,256]{3,1,2,0:T(8,128)(2,1)} %all-gather.5.cloned.1.call-done, bf16[8,64,8,256]{3,2,0,1:T(8,128)(2,1)} %all-gather.3.cloned.1.call-done), kind=kOutput, calls=%fused_computation.5 | convolution fusion | flops 1073741824 | bytes 5242880 | tf_op jit(solution)/shard_map/icka,kbjc->ibja/dot_general | solution.py:15
  86.5 0.0 copy-done
  86.5 0.0 copy-done.4
  86.5 0.0 copy-done.3
  86.5 0.7 fusion.30
  87.2 0.8 copy.12
  88.1 9.5 %psum.7 = f32[2,8]{1,0:T(2,128)S(1)} all-reduce(f32[2,8]{1,0:T(2,128)S(1)} %get-tuple-element.4), channel_id=1, replica_groups=mesh['groups'=2,'occ'=4,'vir'=4] {'vir'}, use_global_device_ids=true, to_apply=%region_1.0 | all-reduce | flops 16 | bytes 128 | tf_op jit(solution)/shard_map/psum | solution.py:33
  97.5 0.6 broadcast_multiply_fusion
  (1 shorter events, 0.0 us)
Async XLA Ops:
  7.2 4.0 %copy-start.2 = (s32[2,8]{1,0:T(2,128)S(1)}, s32[2,8]{1,0:T(2,128)}, u32[]{:S(2)}) copy-start(s32[2,8]{1,0:T(2,128)} %param.11) | copy-start | bytes 196
  7.2 4.0 %copy-start.1 = (f32[256]{0:T(256)S(1)}, f32[256]{0:T(256)}, u32[]{:S(2)}) copy-start(f32[256]{0:T(256)} %param.10) | copy-start | bytes 3076
  7.2 4.1 %copy-start.5 = (f32[8]{0:T(128)S(1)}, f32[8]{0:T(128)}, u32[]{:S(2)}) copy-start(f32[8]{0:T(128)} %param.9) | copy-start | bytes 100
  7.2 27.7 %all-gather.3.cloned.1.call-start = ((), (), s32[]{:S(2)}) async-start(), calls=%async_computation | async-start | bytes 2621440 | tf_op jit(solution)/shard_map/all_gather | solution.py:14
  9.1 73.9 %all-gather.5.cloned.1.call-start = ((), (), s32[]{:S(2)}) async-start(), calls=%async_computation.1 | async-start | bytes 2621440 | tf_op jit(solution)/shard_map/all_gather | solution.py:13
  11.6 74.9 %copy-start = (bf16[2,64,8,256]{3,2,1,0:T(8,128)(2,1)S(1)}, bf16[2,64,8,256]{3,2,1,0:T(8,128)(2,1)}, u32[]{:S(2)}) copy-start(bf16[2,64,8,256]{3,2,1,0:T(8,128)(2,1)} %param.7) | copy-start | bytes 1572868
  11.6 74.9 %copy-start.4 = (bf16[2,8,8,8]{3,2,1,0:T(8,128)(2,1)S(1)}, bf16[2,8,8,8]{3,2,1,0:T(8,128)(2,1)}, u32[]{:S(2)}) copy-start(bf16[2,8,8,8]{3,2,1,0:T(8,128)(2,1)} %param.8) | copy-start | bytes 6148
  34.9 51.6 %copy-start.3 = (bf16[8,64,8,256]{3,2,0,1:T(8,128)(2,1)S(1)}, bf16[8,64,8,256]{3,2,0,1:T(8,128)(2,1)}, u32[]{:S(2)}) copy-start(bf16[8,64,8,256]{3,2,0,1:T(8,128)(2,1)} %all-gather.3.cloned.1.call-done) | copy-start | bytes 6291460
Sparse Core Ops, SparseCore 0:
  9.6 25.2 all-gather.2
  37.0 45.9 all-gather.4
where the time goes:
time: 105 us
  waiting for transfers between devices  71.5 us (68%)
  between operations  14.2 us (14%)
  blocking collectives  9.47 us (9%)
  local copies, waits for them, and re-layouts  4.85 us (5%)
  matrix products  4.18 us (4%)
    all_gather x1, waiting for transfers between devices, per_device(): panel = lax.all_gather(integrals, 'vir', axis=1, tiled=True)  48.1 us
    all_gather x1, waiting for transfers between devices, per_device(): piece = lax.all_gather(amps, 'occ', axis=0, tiled=True)  23.3 us
    psum x1, blocking collectives, per_device(): pair_energy = lax.psum(partial_energy, 'vir') / n_virt  9.47 us
    unnamed x15, local copies, waits for them, and re-layouts  4.69 us
    dot_general x1, matrix products, per_device(): jnp.einsum('icka,kbjc->ibja', panel, piece, preferred_element_type=jnp.fl...  3.47 us
  transfers between devices with their start and end apart: 2, of which 2 were waited for; matrix products, arithmetic and copies ran while one was open for 2% of the time, Pallas kernels for 0%

commit v1 on v0

v1 whole, which is shorter than its diff:
```python
import functools

import jax
import jax.numpy as jnp
from jax import lax
from jax.experimental import pallas as pl
from jax.experimental.pallas import tpu as pltpu
from jax.sharding import PartitionSpec as P

F32, BF16 = jnp.float32, jnp.bfloat16
MESH = pl.DeviceIdType.MESH
TILE = 256
LANES = 128
K_PARTS = 2


def iota(shape, axis):
    return lax.broadcasted_iota(jnp.int32, shape, axis)


def dot(left, right):
    return jnp.dot(left, right, preferred_element_type=F32)


def kernel(
    n_occ, n_vir, nb, n_o,
    a_hbm, g_hbm, w_ref, eo_ref, ev_ref, mask_ref,
    new_hbm, en_ref,
    amps, panel, direct, wblk, acc, rden, newv, eall,
    load_sem, z_send, z_recv, x_send, x_recv, c_send, c_recv, e_send, e_recv, out_sem,
):
    ri, rows, n_v = g_hbm.shape
    n_x = n_occ // 2
    tiles = rows // TILE
    k_per = n_o // K_PARTS
    o_bits = n_o.bit_length() - 1
    chunks = [(i, h) for i in range(ri) for h in range(K_PARTS)]

    z = lax.axis_index("vir")
    m = lax.axis_index("occ")
    sib = m + 1 - 2 * lax.rem(m, 2)
    x_right = lax.rem(m + 2, n_occ)
    x_left = lax.rem(m + n_occ - 2, n_occ)

    def amps_block(origin):
        return amps.at[pl.ds(origin * ri, ri)]

    load_g = [
        pltpu.make_async_copy(g_hbm.at[i], direct.at[i], load_sem.at[i]) for i in range(ri)
    ]
    load_a = pltpu.make_async_copy(a_hbm, amps_block(m), load_sem.at[ri])
    for copy in load_g:
        copy.start()
    load_a.start()

    barrier = pltpu.get_barrier_semaphore()
    for d in range(1, n_vir):
        pl.semaphore_signal(
            barrier, inc=1, device_id={"vir": lax.rem(z + d, n_vir)}, device_id_type=MESH
        )
    for peer in (sib, x_right, x_left):
        pl.semaphore_signal(barrier, inc=1, device_id={"occ": peer}, device_id_type=MESH)

    c_sub = max(TILE // n_o, 16)
    part = c_sub * n_o
    sub_bits = c_sub.bit_length() - 1
    to_row = iota((part, part), 0)
    source = ((to_row & (c_sub - 1)) << o_bits) + (to_row >> sub_bits)
    shuffle = jnp.where(iota((part, part), 1) == source, 1.0, 0.0).astype(BF16)

    def permute(i):
        for s in range(nb // c_sub):
            block = dot(shuffle, direct[i, pl.ds(s * part, part), :]).astype(BF16)
            first = pl.multiple_of(z * nb + s * c_sub, c_sub)
            panel[i, :, pl.ds(first, c_sub), :] = block.reshape(n_o, c_sub, n_v)

    def z_copy(way, origin, q):
        i, h = chunks[q]
        first = pl.multiple_of(origin * nb, nb)
        block = panel.at[i, pl.ds(h * k_per, k_per), pl.ds(first, nb), :]
        target = jnp.clip(z + (1 if way == 0 else -1), 0, n_vir - 1)
        return pltpu.make_async_remote_copy(
            src_ref=block,
            dst_ref=block,
            send_sem=z_send.at[way, origin, q],
            recv_sem=z_recv.at[way, origin, q],
            device_id={"vir": target},
            device_id_type=MESH,
        )

    def has_next(way):
        return z < n_vir - 1 if way == 0 else z > 0

    def origin_of(way, step):
        return z - step if way == 0 else z + step

    def exists(way, step):
        return z - step >= 0 if way == 0 else z + step < n_vir

    def z_start(way, origin, q):
        z_copy(way, origin, q).start()

    def x_copy(step, source=None):
        origin = lax.rem(m + n_occ - 2 * step, n_occ)
        return pltpu.make_async_remote_copy(
            src_ref=amps_block(origin) if source is None else source,
            dst_ref=amps_block(origin),
            send_sem=x_send.at[step],
            recv_sem=x_recv.at[step],
            device_id={"occ": x_right},
            device_id_type=MESH,
        )

    def c_copy(step, source=None):
        origin = lax.rem(m + n_occ - 2 * step, n_occ)
        return pltpu.make_async_remote_copy(
            src_ref=amps_block(origin) if source is None else source,
            dst_ref=amps_block(origin),
            send_sem=c_send.at[step],
            recv_sem=c_recv.at[step],
            device_id={"occ": sib},
            device_id_type=MESH,
        )

    def e_copy(d, i):
        return pltpu.make_async_remote_copy(
            src_ref=eall.at[z, i],
            dst_ref=eall.at[z, i],
            send_sem=e_send.at[d, i],
            recv_sem=e_recv.at[d, i],
            device_id={"vir": lax.rem(z + d, n_vir)},
            device_id_type=MESH,
        )

    def e_arrival(d, i):
        origin = lax.rem(z + n_vir - d, n_vir)
        return pltpu.make_async_remote_copy(
            src_ref=eall.at[origin, i],
            dst_ref=eall.at[origin, i],
            send_sem=e_send.at[d, i],
            recv_sem=e_recv.at[d, i],
            device_id={"vir": origin},
            device_id_type=MESH,
        )

    load_g[0].wait()
    permute(0)
    pl.semaphore_wait(barrier, n_vir + 2)
    for i in range(ri):
        if i:
            load_g[i].wait()
            permute(i)
        for q, (qi, _) in enumerate(chunks):
            if qi == i:
                for way in (0, 1):
                    pl.when(has_next(way))(functools.partial(z_start, way, z, q))
        if i == 0:
            load_a.wait()
            if n_x > 1:
                x_copy(0).start()
            c_copy(0).start()

    row = iota((TILE, 1), 0)
    row_j = row & (n_o - 1)
    eps_j = jnp.zeros((TILE, 1), F32)
    keep = [jnp.zeros((TILE, 1), F32) for _ in range(ri)]
    for j in range(n_o):
        eps_j = jnp.where(row_j == j, eo_ref[j], eps_j)
        for i in range(ri):
            keep[i] = jnp.where(row_j == j, mask_ref[i, j].astype(F32), keep[i])
    ev = ev_ref[...]

    def factors(t, carry):
        own = iota((TILE, n_v), 1) == z * nb + ((t * TILE + iota((TILE, n_v), 0)) >> o_bits)
        eps_b = jnp.sum(jnp.where(own, ev, 0.0), axis=1, keepdims=True)
        for i in range(ri):
            denom = ((ev + eps_b) - eo_ref[m * ri + i]) - eps_j
            rden[i, pl.ds(pl.multiple_of(t * TILE, TILE), TILE), :] = -keep[i] / denom
        return carry

    lax.fori_loop(0, tiles, factors, 0)

    up = jnp.where((iota((TILE, n_o), 0) & (n_o - 1)) == iota((TILE, n_o), 1), 1.0, 0.0)
    across = jnp.where((iota((n_o, TILE), 1) & (n_o - 1)) == iota((n_o, TILE), 0), 1.0, 0.0)
    same_b = (iota((TILE, TILE), 0) >> o_bits) == (iota((TILE, TILE), 1) >> o_bits)
    for i in range(ri):
        w_i = w_ref[i].astype(F32)

        def spread(k, carry, i=i, w_i=w_i):
            w_k = jnp.sum(jnp.where(iota(w_i.shape, 1) == k, w_i, 0.0), axis=1)
            full = dot(up, dot(w_k, across))
            wblk[i, k] = jnp.where(same_b, full, 0.0).astype(BF16)
            return carry

        lax.fori_loop(0, n_o, spread, 0)

    def forward(step, q):
        for way in (0, 1):

            def take(way=way):
                z_copy(way, origin_of(way, step), q).wait_recv()
                pl.when(has_next(way))(
                    functools.partial(z_start, way, origin_of(way, step), q)
                )

            pl.when(exists(way, step))(take)

    def rows_of(t):
        return pl.ds(pl.multiple_of(t * TILE, TILE), TILE)

    def ladder(i):
        def body(t, carry):
            value = direct[i, rows_of(t), :].astype(F32)

            def add(k8, value):
                for kk in range(8):
                    k = k8 * 8 + kk
                    value = value + dot(wblk[i, k], amps[k, rows_of(t), :])
                return value

            acc[i, rows_of(t), :] = lax.fori_loop(0, n_o // 8, add, value)
            return carry

        lax.fori_loop(0, tiles, body, 0)

    def cycle(q, last):
        i, h = chunks[q]

        def body(t, carry):
            value = acc[i, rows_of(t), :]

            def add(k4, value):
                for kk in range(4):
                    k = h * k_per + k4 * 4 + kk
                    value = value + dot(amps[k, rows_of(t), :], panel[i, k])
                return value

            value = lax.fori_loop(0, k_per // 4, add, value)
            if not last:
                acc[i, rows_of(t), :] = value
                return carry
            new = (value * rden[i, rows_of(t), :]).astype(BF16)
            newv[i, rows_of(t), :] = new
            prod = direct[i, rows_of(t), :].astype(F32) * new.astype(F32)
            return carry + jnp.sum(prod.reshape(TILE // n_o, n_o, n_v), axis=0)

        if not last:
            lax.fori_loop(0, tiles, body, 0)
            return
        energy = lax.fori_loop(0, tiles, body, jnp.zeros((n_o, n_v), F32))
        out = pltpu.make_async_copy(newv.at[i], new_hbm.at[i], out_sem.at[i])
        out.start()
        folded = energy[:, :LANES]
        for s in range(1, n_v // LANES):
            folded = folded + energy[:, s * LANES : (s + 1) * LANES]
        eall[z, i] = folded
        for d in range(1, n_vir):
            e_copy(d, i).start()

    def amps_step(step):
        if step:
            x_copy(step - 1).wait_recv()
            if step < n_x - 1:
                x_copy(step).start()
            c_copy(step).start()

    work = [functools.partial(amps_step, s) for s in range(1, n_x)]

    def all_amps():
        for s in range(n_x):
            c_copy(s).wait_recv()

    tail_work = [all_amps] + [functools.partial(ladder, i) for i in range(ri)]
    slots = []
    for step in range(1, n_vir - 1):
        for q in range(len(chunks)):
            slots.append((step, q))
    for index, (step, q) in enumerate(slots):
        forward(step, q)
        if work:
            work.pop(0)()
        elif index >= len(chunks) and tail_work:
            tail_work.pop(0)()
    for piece in work + tail_work:
        piece()
    for q, (i, h) in enumerate(chunks):
        forward(n_vir - 1, q)
        cycle(q, h == K_PARTS - 1)

    for i in range(ri):
        for d in range(1, n_vir):
            e_arrival(d, i).wait_recv()
        total = eall[0, i]
        for s in range(1, n_vir):
            total = total + eall[s, i]
        column = jnp.sum(total, axis=1, keepdims=True) / n_v
        spot = iota((n_o, LANES), 0) == iota((n_o, LANES), 1)
        line = jnp.sum(jnp.where(spot, column, 0.0), axis=0, keepdims=True)
        en_ref[pl.ds(i, 1), :] = line[:, :n_o]

    for way in (0, 1):
        for step in range(n_vir):
            for q in range(len(chunks)):

                def sent(way=way, step=step, q=q):
                    z_copy(way, origin_of(way, step), q).wait_send()

                pl.when(jnp.logical_and(has_next(way), exists(way, step)))(sent)
    for s in range(n_x):
        if s < n_x - 1:
            x_copy(s).wait_send()
        c_copy(s).wait_send()
    for i in range(ri):
        for d in range(1, n_vir):
            e_copy(d, i).wait_send()
        pltpu.make_async_copy(newv.at[i], new_hbm.at[i], out_sem.at[i]).wait()


def per_device(n_occ, n_vir, amps, integrals, ladder_ints, eps_occ, eps_vir, pair_mask):
    ri, nb, n_o, n_v = amps.shape
    rows = nb * n_o
    n_chunks = ri * K_PARTS
    n_x = n_occ // 2
    flops = 2 * 2 * ri * rows * n_v * n_o * n_v
    dma = pltpu.SemaphoreType.DMA
    new, energy = pl.pallas_call(
        functools.partial(kernel, n_occ, n_vir, nb, n_o),
        out_shape=(
            jax.ShapeDtypeStruct((ri, rows, n_v), BF16),
            jax.ShapeDtypeStruct((ri, n_o), F32),
        ),
        in_specs=[
            pl.BlockSpec(memory_space=pl.ANY),
            pl.BlockSpec(memory_space=pl.ANY),
            pl.BlockSpec(memory_space=pltpu.VMEM),
            pl.BlockSpec(memory_space=pltpu.SMEM),
            pl.BlockSpec(memory_space=pltpu.VMEM),
            pl.BlockSpec(memory_space=pltpu.SMEM),
        ],
        out_specs=(
            pl.BlockSpec(memory_space=pl.ANY),
            pl.BlockSpec(memory_space=pltpu.VMEM),
        ),
        scratch_shapes=[
            pltpu.VMEM((n_o, rows, n_v), BF16),
            pltpu.VMEM((ri, n_o, n_v, n_v), BF16),
            pltpu.VMEM((ri, rows, n_v), BF16),
            pltpu.VMEM((ri, n_o, TILE, TILE), BF16),
            pltpu.VMEM((ri, rows, n_v), F32),
            pltpu.VMEM((ri, rows, n_v), F32),
            pltpu.VMEM((ri, rows, n_v), BF16),
            pltpu.VMEM((n_vir, ri, n_o, LANES), F32),
            dma((ri + 1,)),
            dma((2, n_vir, n_chunks)),
            dma((2, n_vir, n_chunks)),
            dma((n_x,)),
            dma((n_x,)),
            dma((n_x,)),
            dma((n_x,)),
            dma((n_vir, ri)),
            dma((n_vir, ri)),
            dma((ri,)),
        ],
        compiler_params=pltpu.CompilerParams(
            collective_id=0, has_side_effects=True, vmem_limit_bytes=56 * 2**20
        ),
        cost_estimate=pl.CostEstimate(
            flops=flops, bytes_accessed=3 * ri * rows * n_v * 2, transcendentals=0
        ),
    )(
        amps.reshape(ri, rows, n_v),
        integrals.reshape(ri, rows, n_v),
        ladder_ints,
        eps_occ,
        eps_vir.reshape(1, n_v),
        pair_mask,
    )
    return new.reshape(ri, nb, n_o, n_v), energy


def solution(mesh):
    in_specs = (
        P(("groups", "occ"), "vir", None, None),
        P(("groups", "occ"), "vir", None, None),
        P(("groups", "occ"), None, None, None),
        P("groups"),
        P("groups"),
        P(("groups", "occ"), None),
    )
    out_specs = (P(("groups", "occ"), "vir", None, None), P(("groups", "occ"), None))
    body = functools.partial(per_device, mesh.shape["occ"], mesh.shape["vir"])
    return jax.shard_map(
        body, mesh=mesh, in_specs=in_specs, out_specs=out_specs, check_vma=False
    )
```

time: 105 us -> 49.4 us (0.47)
  waiting for transfers between devices: 71.5 us -> 0 us
  Pallas kernels: 0 us -> 46.1 us
  between operations: 14.2 us -> 0.65 us
  blocking collectives: 9.47 us -> 0 us
  matrix products: 4.18 us -> 0 us
  local copies, waits for them, and re-layouts: 4.85 us -> 2.44 us
    all_gather x2 -> x0, waiting for transfers between devices: 71.4 us -> none  [the longest x1 48.1 us: per_device(): panel = lax.all_gather(integrals, 'vir', axis=1, tiled=True)]
    pallas_call x0 -> x1, Pallas kernels: none -> 46.1 us  [per_device(): pl.pallas_call(functools.partial(kernel, n_occ, n_vir, nb, n_o), out_shap...]
    psum x1 -> x0, blocking collectives: 9.47 us -> none  [per_device(): pair_energy = lax.psum(partial_energy, 'vir') / n_virt]
    dot_general x2 -> x0, matrix products: 4.18 us -> none  [the longest x1 3.47 us: per_device(): jnp.einsum('icka,kbjc->ibja', panel, piece, preferred_element_type=jnp.fl...]
    unnamed x15 -> x4, local copies, waits for them, and re-layouts: 4.69 us -> 2.44 us
  transfers between devices with their start and end apart: 2 -> 0, of which waited for: 2 -> 0; matrix products, arithmetic and copies ran while one was open for 2% -> 0% of each run, Pallas kernels for 0% -> 0%
where the time goes in v1:
time: 49.4 us; the launch traced here: 49.2 us
  Pallas kernels  46.1 us (93%)
  local copies, waits for them, and re-layouts  2.44 us (5%)
  between operations  0.65 us (1%)
    pallas_call x1, Pallas kernels, per_device(): pl.pallas_call(functools.partial(kernel, n_occ, n_vir, nb, n_o), out_shap...  46.1 us
    unnamed x4, local copies, waits for them, and re-layouts  2.44 us

profile of v1, /device:TPU:0, one launch (start us, length us, event | category | flops | bytes accessed | tf_op | source)
XLA Modules:
  0.0 49.2 jit_solution(5620457683155313143)
XLA Ops:
  0.6 46.1 %shard_map.77 = (bf16[2,512,256]{2,1,0:T(8,128)(2,1)}, f32[2,8]{1,0:T(2,128)}) custom-call(bf16[2,512,256]{2,1,0:T(8,128)(2,1)} %bitcast.5, bf16[2,512,256]{2,1,0:T(8,128)(2,1)} %bitcast.6, bf16[2,8,8,8]{3,2,1,0:T(8,128)(2,1)} %w_ref.1, f32[8]{0:T(128)} %eo_ref.1, f32[1,256]{1,0:T(1,128)} %bitcast.7, s32[2,8]{1,0:T(2,128)} %mask_ref.1), custom_call_target="tpu_custom_call" | custom-call | flops 2147483648 | bytes 1572864 | tf_op jit(solution)/shard_map/pallas_call | solution.py:326
  46.8 0.0 copy-start
  46.8 1.9 %copy.10 = bf16[2,64,8,256]{3,2,1,0:T(8,128)(2,1)} copy(bf16[2,64,8,256]{3,2,1,0:T(8,128)(2,1)} %bitcast.4) | data formatting | bytes 1048576
  48.6 0.0 copy-done
  48.6 0.6 %copy.11 = f32[2,8]{1,0:T(2,128)} copy(f32[2,8]{1,0:T(2,128)S(1)} %copy-done) | data formatting | bytes 128
Async XLA Ops:
  46.8 1.9 %copy-start = (f32[2,8]{1,0:T(2,128)S(1)}, f32[2,8]{1,0:T(2,128)}, u32[]{:S(2)}) copy-start(f32[2,8]{1,0:T(2,128)} %get-tuple-element.9) | copy-start | bytes 196

commit v2 on v1

--- a/solution.py
+++ b/solution.py
@@ -23,11 +23,13 @@
 
 
 def kernel(
-    n_occ, n_vir, nb, n_o,
+    n_occ, n_vir, nb, n_o, lend,
     a_hbm, g_hbm, w_ref, eo_ref, ev_ref, mask_ref,
     new_hbm, en_ref,
     amps, panel, direct, wblk, acc, rden, newv, eall,
+    amps2, direct2, rden2, new2,
     load_sem, z_send, z_recv, x_send, x_recv, c_send, c_recv, e_send, e_recv, out_sem,
+    t_send, t_recv, tx_send, tx_recv, tc_send, tc_recv, r_send, r_recv,
 ):
     ri, rows, n_v = g_hbm.shape
     n_x = n_occ // 2
@@ -88,14 +90,92 @@
             device_id_type=MESH,
         )
 
-    def has_next(way):
-        return z < n_vir - 1 if way == 0 else z > 0
+    last = ri - 1
+    is_end = jnp.logical_or(z == 0, z == n_vir - 1)
+    is_helper = jnp.logical_or(z == 1, z == n_vir - 2)
+    low_half = z < n_vir // 2
+    z_in = jnp.where(low_half, z + 1, z - 1)
+    z_out = jnp.clip(jnp.where(low_half, z - 1, z + 1), 0, n_vir - 1)
+
+    def lent(q):
+        return lend and chunks[q][0] == last
+
+    def has_next(way, q):
+        margin = 1 if lent(q) else 0
+        return z < n_vir - 1 - margin if way == 0 else z > margin
 
     def origin_of(way, step):
         return z - step if way == 0 else z + step
 
-    def exists(way, step):
-        return z - step >= 0 if way == 0 else z + step < n_vir
+    def exists(way, step, q):
+        there = z - step >= 0 if way == 0 else z + step < n_vir
+        if lent(q) and step:
+            there = jnp.logical_and(there, jnp.logical_not(is_end))
+        return there
+
+    def block2(origin, t):
+        return amps2.at[pl.ds(origin * ri, ri), pl.ds(t * TILE, TILE), :]
+
+    def t_copy(t):
+        return pltpu.make_async_remote_copy(
+            src_ref=amps.at[pl.ds(m * ri, ri), pl.ds(t * TILE, TILE), :],
+            dst_ref=block2(m, t),
+            send_sem=t_send.at[t],
+            recv_sem=t_recv.at[t],
+            device_id={"vir": z_in},
+            device_id_type=MESH,
+        )
+
+    def tx_copy(step, t):
+        block = block2(lax.rem(m + n_occ - 2 * step, n_occ), t)
+        return pltpu.make_async_remote_copy(
+            src_ref=block,
+            dst_ref=block,
+            send_sem=tx_send.at[step, t],
+            recv_sem=tx_recv.at[step, t],
+            device_id={"occ": x_right},
+            device_id_type=MESH,
+        )
+
+    def tc_copy(step, t):
+        block = block2(lax.rem(m + n_occ - 2 * step, n_occ), t)
+        return pltpu.make_async_remote_copy(
+            src_ref=block,
+            dst_ref=block,
+            send_sem=tc_send.at[step, t],
+            recv_sem=tc_recv.at[step, t],
+            device_id={"occ": sib},
+            device_id_type=MESH,
+        )
+
+    def r_copy(t):
+        return pltpu.make_async_remote_copy(
+            src_ref=new2.at[pl.ds(t * TILE, TILE), :],
+            dst_ref=newv.at[last, pl.ds(t * TILE, TILE), :],
+            send_sem=r_send.at[t],
+            recv_sem=r_recv.at[t],
+            device_id={"vir": z_out},
+            device_id_type=MESH,
+        )
+
+    def lend_amps():
+        for t in range(tiles):
+            t_copy(t).start()
+
+    def helper_take():
+        for t in range(tiles):
+            t_copy(t).wait_recv()
+            if n_x > 1:
+                tx_copy(0, t).start()
+            tc_copy(0, t).start()
+
+    def helper_x():
+        for step in range(1, n_x):
+            for t in range(tiles):
+                tx_copy(step - 1, t).wait_recv()
+                if step < n_x - 1:
+                    tx_copy(step, t).start()
+                tc_copy(step, t).start()
 
     def z_start(way, origin, q):
         z_copy(way, origin, q).start()
@@ -153,12 +233,14 @@
         for q, (qi, _) in enumerate(chunks):
             if qi == i:
                 for way in (0, 1):
-                    pl.when(has_next(way))(functools.partial(z_start, way, z, q))
+                    pl.when(has_next(way, q))(functools.partial(z_start, way, z, q))
         if i == 0:
             load_a.wait()
             if n_x > 1:
                 x_copy(0).start()
             c_copy(0).start()
+            if lend:
+                pl.when(is_end)(lend_amps)
 
     row = iota((TILE, 1), 0)
     row_j = row & (n_o - 1)
@@ -180,6 +262,18 @@
 
     lax.fori_loop(0, tiles, factors, 0)
 
+    def factors2(t, carry):
+        own = iota((TILE, n_v), 1) == z_out * nb + (
+            (t * TILE + iota((TILE, n_v), 0)) >> o_bits
+        )
+        eps_b = jnp.sum(jnp.where(own, ev, 0.0), axis=1, keepdims=True)
+        denom = ((ev + eps_b) - eo_ref[m * ri + last]) - eps_j
+        rden2[pl.ds(pl.multiple_of(t * TILE, TILE), TILE), :] = -keep[last] / denom
+        return carry
+
+    if lend:
+        lax.fori_loop(0, tiles, factors2, 0)
+
     up = jnp.where((iota((TILE, n_o), 0) & (n_o - 1)) == iota((TILE, n_o), 1), 1.0, 0.0)
     across = jnp.where((iota((n_o, TILE), 1) & (n_o - 1)) == iota((n_o, TILE), 0), 1.0, 0.0)
     same_b = (iota((TILE, TILE), 0) >> o_bits) == (iota((TILE, TILE), 1) >> o_bits)
@@ -199,11 +293,11 @@
 
             def take(way=way):
                 z_copy(way, origin_of(way, step), q).wait_recv()
-                pl.when(has_next(way))(
+                pl.when(has_next(way, q))(
                     functools.partial(z_start, way, origin_of(way, step), q)
                 )
 
-            pl.when(exists(way, step))(take)
+            pl.when(exists(way, step, q))(take)
 
     def rows_of(t):
         return pl.ds(pl.multiple_of(t * TILE, TILE), TILE)
@@ -247,7 +341,9 @@
         if not last:
             lax.fori_loop(0, tiles, body, 0)
             return
-        energy = lax.fori_loop(0, tiles, body, jnp.zeros((n_o, n_v), F32))
+        finish(i, lax.fori_loop(0, tiles, body, jnp.zeros((n_o, n_v), F32)))
+
+    def finish(i, energy):
         out = pltpu.make_async_copy(newv.at[i], new_hbm.at[i], out_sem.at[i])
         out.start()
         folded = energy[:, :LANES]
@@ -257,6 +353,41 @@
         for d in range(1, n_vir):
             e_copy(d, i).start()
 
+    def helper_rows():
+        from_row = iota((part, part), 1)
+        place = ((from_row & (c_sub - 1)) << o_bits) + (from_row >> sub_bits)
+        back = jnp.where(iota((part, part), 0) == place, 1.0, 0.0).astype(BF16)
+        for s in range(nb // c_sub):
+            first = pl.multiple_of(z_out * nb + s * c_sub, c_sub)
+            block = panel[last, :, pl.ds(first, c_sub), :].reshape(part, n_v)
+            direct2[pl.ds(s * part, part), :] = dot(back, block).astype(BF16)
+        for step in range(n_x):
+            for t in range(tiles):
+                tc_copy(step, t).wait_recv()
+        for t in range(tiles):
+            here = pl.ds(t * TILE, TILE)
+
+            def add(k4, value, here=here):
+                for kk in range(4):
+                    k = k4 * 4 + kk
+                    rows_k = amps2[k, here, :]
+                    value = value + dot(wblk[last, k], rows_k)
+                    value = value + dot(rows_k, panel[last, k])
+                return value
+
+            value = lax.fori_loop(0, n_o // 4, add, direct2[here, :].astype(F32))
+            new2[here, :] = (value * rden2[here, :]).astype(BF16)
+            r_copy(t).start()
+
+    def end_rows():
+        energy = jnp.zeros((n_o, n_v), F32)
+        for t in range(tiles):
+            here = pl.ds(t * TILE, TILE)
+            r_copy(t).wait_recv()
+            prod = direct[last, here, :].astype(F32) * newv[last, here, :].astype(F32)
+            energy = energy + jnp.sum(prod.reshape(TILE // n_o, n_o, n_v), axis=0)
+        finish(last, energy)
+
     def amps_step(step):
         if step:
             x_copy(step - 1).wait_recv()
@@ -264,28 +395,42 @@
                 x_copy(step).start()
             c_copy(step).start()
 
-    work = [functools.partial(amps_step, s) for s in range(1, n_x)]
-
     def all_amps():
         for s in range(n_x):
             c_copy(s).wait_recv()
 
-    tail_work = [all_amps] + [functools.partial(ladder, i) for i in range(ri)]
-    slots = []
+    def helper_piece(piece):
+        if lend:
+            pl.when(is_helper)(piece)
+
+    def ladder_piece(i):
+        if lend and i == last:
+            pl.when(jnp.logical_not(is_end))(functools.partial(ladder, i))
+        else:
+            ladder(i)
+
+    work = [functools.partial(amps_step, s) for s in range(1, n_x)]
+    work += [functools.partial(helper_piece, helper_x), all_amps]
+    work += [functools.partial(ladder_piece, i) for i in range(ri)]
     for step in range(1, n_vir - 1):
         for q in range(len(chunks)):
-            slots.append((step, q))
-    for index, (step, q) in enumerate(slots):
-        forward(step, q)
-        if work:
-            work.pop(0)()
-        elif index >= len(chunks) and tail_work:
-            tail_work.pop(0)()
-    for piece in work + tail_work:
+            if step == 1 and lent(q) and not lent(q - 1):
+                helper_piece(helper_take)
+            forward(step, q)
+            if (step > 1 or q == len(chunks) - 1) and work:
+                work.pop(0)()
+    for piece in work:
         piece()
+    helper_piece(helper_rows)
     for q, (i, h) in enumerate(chunks):
         forward(n_vir - 1, q)
-        cycle(q, h == K_PARTS - 1)
+        piece = functools.partial(cycle, q, h == K_PARTS - 1)
+        if lent(q):
+            pl.when(jnp.logical_not(is_end))(piece)
+        else:
+            piece()
+    if lend:
+        pl.when(is_end)(end_rows)
 
     for i in range(ri):
         for d in range(1, n_vir):
@@ -305,11 +450,26 @@
                 def sent(way=way, step=step, q=q):
                     z_copy(way, origin_of(way, step), q).wait_send()
 
-                pl.when(jnp.logical_and(has_next(way), exists(way, step)))(sent)
+                pl.when(jnp.logical_and(has_next(way, q), exists(way, step, q)))(sent)
     for s in range(n_x):
         if s < n_x - 1:
             x_copy(s).wait_send()
         c_copy(s).wait_send()
+    def helper_sent():
+        for t in range(tiles):
+            for s in range(n_x):
+                if s < n_x - 1:
+                    tx_copy(s, t).wait_send()
+                tc_copy(s, t).wait_send()
+            r_copy(t).wait_send()
+
+    def end_sent():
+        for t in range(tiles):
+            t_copy(t).wait_send()
+
+    if lend:
+        pl.when(is_helper)(helper_sent)
+        pl.when(is_end)(end_sent)
     for i in range(ri):
         for d in range(1, n_vir):
             e_copy(d, i).wait_send()
@@ -323,8 +483,11 @@
     n_x = n_occ // 2
     flops = 2 * 2 * ri * rows * n_v * n_o * n_v
     dma = pltpu.SemaphoreType.DMA
+    tiles = rows // TILE
+    lend = n_vir >= 4 and n_o * rows * n_v * 2 <= 4 * 2**20
+    extra = rows if lend else 16
     new, energy = pl.pallas_call(
-        functools.partial(kernel, n_occ, n_vir, nb, n_o),
+        functools.partial(kernel, n_occ, n_vir, nb, n_o, lend),
         out_shape=(
             jax.ShapeDtypeStruct((ri, rows, n_v), BF16),
             jax.ShapeDtypeStruct((ri, n_o), F32),
@@ -350,6 +513,10 @@
             pltpu.VMEM((ri, rows, n_v), F32),
             pltpu.VMEM((ri, rows, n_v), BF16),
             pltpu.VMEM((n_vir, ri, n_o, LANES), F32),
+            pltpu.VMEM((n_o, extra, n_v), BF16),
+            pltpu.VMEM((extra, n_v), BF16),
+            pltpu.VMEM((extra, n_v), F32),
+            pltpu.VMEM((extra, n_v), BF16),
             dma((ri + 1,)),
             dma((2, n_vir, n_chunks)),
             dma((2, n_vir, n_chunks)),
@@ -360,6 +527,14 @@
             dma((n_vir, ri)),
             dma((n_vir, ri)),
             dma((ri,)),
+            dma((tiles,)),
+            dma((tiles,)),
+            dma((n_x, tiles)),
+            dma((n_x, tiles)),
+            dma((n_x, tiles)),
+            dma((n_x, tiles)),
+            dma((tiles,)),
+            dma((tiles,)),
         ],
         compiler_params=pltpu.CompilerParams(
             collective_id=0, has_side_effects=True, vmem_limit_bytes=56 * 2**20

time: 49.4 us -> 51.9 us (1.051)
  Pallas kernels: 46.1 us -> 48.6 us
    pallas_call x1, Pallas kernels: 46.1 us -> 48.6 us  [per_device(): pl.pallas_call(functools.partial(kernel, n_occ, n_vir, nb, n_o, lend), ou...]
where the time goes in v2:
time: 51.9 us; the launch traced here: 51.7 us
  Pallas kernels  48.6 us (94%)
  local copies, waits for them, and re-layouts  2.44 us (5%)
  between operations  0.65 us (1%)
    pallas_call x1, Pallas kernels, per_device(): pl.pallas_call(functools.partial(kernel, n_occ, n_vir, nb, n_o, lend), ou...  48.6 us
    unnamed x4, local copies, waits for them, and re-layouts  2.44 us

profile of v2, /device:TPU:0, one launch (start us, length us, event | category | flops | bytes accessed | tf_op | source)
XLA Modules:
  0.0 51.7 jit_solution(15307451998279160527)
XLA Ops:
  0.6 48.6 %shard_map.77 = (bf16[2,512,256]{2,1,0:T(8,128)(2,1)}, f32[2,8]{1,0:T(2,128)}) custom-call(bf16[2,512,256]{2,1,0:T(8,128)(2,1)} %bitcast.5, bf16[2,512,256]{2,1,0:T(8,128)(2,1)} %bitcast.6, bf16[2,8,8,8]{3,2,1,0:T(8,128)(2,1)} %w_ref.1, f32[8]{0:T(128)} %eo_ref.1, f32[1,256]{1,0:T(1,128)} %bitcast.7, s32[2,8]{1,0:T(2,128)} %mask_ref.1), custom_call_target="tpu_custom_call" | custom-call | flops 2147483648 | bytes 1572864 | tf_op jit(solution)/shard_map/pallas_call | solution.py:489
  49.3 0.0 copy-start
  49.3 1.9 %copy.10 = bf16[2,64,8,256]{3,2,1,0:T(8,128)(2,1)} copy(bf16[2,64,8,256]{3,2,1,0:T(8,128)(2,1)} %bitcast.4) | data formatting | bytes 1048576
  51.2 0.0 copy-done
  51.2 0.6 %copy.11 = f32[2,8]{1,0:T(2,128)} copy(f32[2,8]{1,0:T(2,128)S(1)} %copy-done) | data formatting | bytes 128
Async XLA Ops:
  49.3 1.9 %copy-start = (f32[2,8]{1,0:T(2,128)S(1)}, f32[2,8]{1,0:T(2,128)}, u32[]{:S(2)}) copy-start(f32[2,8]{1,0:T(2,128)} %get-tuple-element.9) | copy-start | bytes 196

commit v3 on v2

--- a/solution.py
+++ b/solution.py
@@ -12,6 +12,7 @@
 TILE = 256
 LANES = 128
 K_PARTS = 2
+STRIP = 128
 
 
 def iota(shape, axis):
@@ -34,6 +35,7 @@
     ri, rows, n_v = g_hbm.shape
     n_x = n_occ // 2
     tiles = rows // TILE
+    strips = rows // STRIP
     k_per = n_o // K_PARTS
     o_bits = n_o.bit_length() - 1
     chunks = [(i, h) for i in range(ri) for h in range(K_PARTS)]
@@ -114,11 +116,11 @@
         return there
 
     def block2(origin, t):
-        return amps2.at[pl.ds(origin * ri, ri), pl.ds(t * TILE, TILE), :]
+        return amps2.at[pl.ds(origin * ri, ri), pl.ds(t * STRIP, STRIP), :]
 
     def t_copy(t):
         return pltpu.make_async_remote_copy(
-            src_ref=amps.at[pl.ds(m * ri, ri), pl.ds(t * TILE, TILE), :],
+            src_ref=amps.at[pl.ds(m * ri, ri), pl.ds(t * STRIP, STRIP), :],
             dst_ref=block2(m, t),
             send_sem=t_send.at[t],
             recv_sem=t_recv.at[t],
@@ -150,8 +152,8 @@
 
     def r_copy(t):
         return pltpu.make_async_remote_copy(
-            src_ref=new2.at[pl.ds(t * TILE, TILE), :],
-            dst_ref=newv.at[last, pl.ds(t * TILE, TILE), :],
+            src_ref=new2.at[pl.ds(t * STRIP, STRIP), :],
+            dst_ref=newv.at[last, pl.ds(t * STRIP, STRIP), :],
             send_sem=r_send.at[t],
             recv_sem=r_recv.at[t],
             device_id={"vir": z_out},
@@ -159,23 +161,21 @@
         )
 
     def lend_amps():
-        for t in range(tiles):
+        for t in range(strips):
             t_copy(t).start()
 
-    def helper_take():
-        for t in range(tiles):
-            t_copy(t).wait_recv()
-            if n_x > 1:
-                tx_copy(0, t).start()
-            tc_copy(0, t).start()
-
-    def helper_x():
+    def helper_take(t):
+        t_copy(t).wait_recv()
+        if n_x > 1:
+            tx_copy(0, t).start()
+        tc_copy(0, t).start()
+
+    def helper_x(t):
         for step in range(1, n_x):
-            for t in range(tiles):
-                tx_copy(step - 1, t).wait_recv()
-                if step < n_x - 1:
-                    tx_copy(step, t).start()
-                tc_copy(step, t).start()
+            tx_copy(step - 1, t).wait_recv()
+            if step < n_x - 1:
+                tx_copy(step, t).start()
+            tc_copy(step, t).start()
 
     def z_start(way, origin, q):
         z_copy(way, origin, q).start()
@@ -226,6 +226,9 @@
     load_g[0].wait()
     permute(0)
     pl.semaphore_wait(barrier, n_vir + 2)
+    if lend:
+        load_a.wait()
+        pl.when(is_end)(lend_amps)
     for i in range(ri):
         if i:
             load_g[i].wait()
@@ -235,12 +238,11 @@
                 for way in (0, 1):
                     pl.when(has_next(way, q))(functools.partial(z_start, way, z, q))
         if i == 0:
-            load_a.wait()
+            if not lend:
+                load_a.wait()
             if n_x > 1:
                 x_copy(0).start()
             c_copy(0).start()
-            if lend:
-                pl.when(is_end)(lend_amps)
 
     row = iota((TILE, 1), 0)
     row_j = row & (n_o - 1)
@@ -288,8 +290,15 @@
 
         lax.fori_loop(0, n_o, spread, 0)
 
-    def forward(step, q):
+    def forward(step, q, side=None):
         for way in (0, 1):
+            inner = low_half if way == 1 else jnp.logical_not(low_half)
+            now = exists(way, step, q)
+            if side == "in":
+                now = jnp.logical_and(now, jnp.logical_or(jnp.logical_not(is_helper), inner))
+            if side == "out":
+                outer = jnp.logical_and(is_helper, jnp.logical_not(inner))
+                now = jnp.logical_and(now, outer)
 
             def take(way=way):
                 z_copy(way, origin_of(way, step), q).wait_recv()
@@ -297,7 +306,7 @@
                     functools.partial(z_start, way, origin_of(way, step), q)
                 )
 
-            pl.when(exists(way, step, q))(take)
+            pl.when(now)(take)
 
     def rows_of(t):
         return pl.ds(pl.multiple_of(t * TILE, TILE), TILE)
@@ -361,17 +370,20 @@
             first = pl.multiple_of(z_out * nb + s * c_sub, c_sub)
             block = panel[last, :, pl.ds(first, c_sub), :].reshape(part, n_v)
             direct2[pl.ds(s * part, part), :] = dot(back, block).astype(BF16)
-        for step in range(n_x):
-            for t in range(tiles):
+
+        for t in range(strips):
+            ahead = t + 2
+            if ahead < strips:
+                helper_x(ahead)
+            for step in range(n_x):
                 tc_copy(step, t).wait_recv()
-        for t in range(tiles):
-            here = pl.ds(t * TILE, TILE)
+            here = pl.ds(t * STRIP, STRIP)
 
             def add(k4, value, here=here):
                 for kk in range(4):
                     k = k4 * 4 + kk
                     rows_k = amps2[k, here, :]
-                    value = value + dot(wblk[last, k], rows_k)
+                    value = value + dot(wblk[last, k, :STRIP, :STRIP], rows_k)
                     value = value + dot(rows_k, panel[last, k])
                 return value
 
@@ -381,11 +393,11 @@
 
     def end_rows():
         energy = jnp.zeros((n_o, n_v), F32)
-        for t in range(tiles):
-            here = pl.ds(t * TILE, TILE)
+        for t in range(strips):
+            here = pl.ds(t * STRIP, STRIP)
             r_copy(t).wait_recv()
             prod = direct[last, here, :].astype(F32) * newv[last, here, :].astype(F32)
-            energy = energy + jnp.sum(prod.reshape(TILE // n_o, n_o, n_v), axis=0)
+            energy = energy + jnp.sum(prod.reshape(STRIP // n_o, n_o, n_v), axis=0)
         finish(last, energy)
 
     def amps_step(step):
@@ -409,18 +421,40 @@
         else:
             ladder(i)
 
-    work = [functools.partial(amps_step, s) for s in range(1, n_x)]
-    work += [functools.partial(helper_piece, helper_x), all_amps]
-    work += [functools.partial(ladder_piece, i) for i in range(ri)]
-    for step in range(1, n_vir - 1):
-        for q in range(len(chunks)):
-            if step == 1 and lent(q) and not lent(q - 1):
-                helper_piece(helper_take)
-            forward(step, q)
-            if (step > 1 or q == len(chunks) - 1) and work:
-                work.pop(0)()
-    for piece in work:
-        piece()
+    if lend:
+        n_q = len(chunks)
+        for q in range(max(n_q, strips)):
+            if q < n_q:
+                forward(1, q, "in")
+            if q < strips:
+                helper_piece(functools.partial(helper_take, q))
+        for s in range(1, n_x):
+            amps_step(s)
+        for step in range(2, n_vir - 1):
+            for q in range(n_q):
+                if step == 2:
+                    forward(1, q, "out")
+                forward(step, q)
+                if step > 2:
+                    continue
+                if q == 1:
+                    all_amps()
+                    ladder_piece(0)
+                    helper_piece(functools.partial(helper_x, 0))
+                if q == 2:
+                    for i in range(1, ri):
+                        ladder_piece(i)
+                    helper_piece(functools.partial(helper_x, 1))
+    else:
+        work = [functools.partial(amps_step, s) for s in range(1, n_x)] + [all_amps]
+        work += [functools.partial(ladder_piece, i) for i in range(ri)]
+        for step in range(1, n_vir - 1):
+            for q in range(len(chunks)):
+                forward(step, q)
+                if (step > 1 or q == len(chunks) - 1) and work:
+                    work.pop(0)()
+        for piece in work:
+            piece()
     helper_piece(helper_rows)
     for q, (i, h) in enumerate(chunks):
         forward(n_vir - 1, q)
@@ -456,7 +490,7 @@
             x_copy(s).wait_send()
         c_copy(s).wait_send()
     def helper_sent():
-        for t in range(tiles):
+        for t in range(strips):
             for s in range(n_x):
                 if s < n_x - 1:
                     tx_copy(s, t).wait_send()
@@ -464,7 +498,7 @@
             r_copy(t).wait_send()
 
     def end_sent():
-        for t in range(tiles):
+        for t in range(strips):
             t_copy(t).wait_send()
 
     if lend:
@@ -483,14 +517,14 @@
     n_x = n_occ // 2
     flops = 2 * 2 * ri * rows * n_v * n_o * n_v
     dma = pltpu.SemaphoreType.DMA
-    tiles = rows // TILE
+    strips = rows // STRIP
     lend = n_vir >= 4 and n_o * rows * n_v * 2 <= 4 * 2**20
     extra = rows if lend else 16
     new, energy = pl.pallas_call(
         functools.partial(kernel, n_occ, n_vir, nb, n_o, lend),
         out_shape=(
-            jax.ShapeDtypeStruct((ri, rows, n_v), BF16),
-            jax.ShapeDtypeStruct((ri, n_o), F32),
+            pltpu.VMEM((ri, rows, n_v), BF16),
+            pltpu.VMEM((ri, n_o), F32),
         ),
         in_specs=[
             pl.BlockSpec(memory_space=pl.ANY),
@@ -501,7 +535,7 @@
             pl.BlockSpec(memory_space=pltpu.SMEM),
         ],
         out_specs=(
-            pl.BlockSpec(memory_space=pl.ANY),
+            pl.BlockSpec(memory_space=pltpu.VMEM),
             pl.BlockSpec(memory_space=pltpu.VMEM),
         ),
         scratch_shapes=[
@@ -527,14 +561,14 @@
             dma((n_vir, ri)),
             dma((n_vir, ri)),
             dma((ri,)),
-            dma((tiles,)),
-            dma((tiles,)),
-            dma((n_x, tiles)),
-            dma((n_x, tiles)),
-            dma((n_x, tiles)),
-            dma((n_x, tiles)),
-            dma((tiles,)),
-            dma((tiles,)),
+            dma((strips,)),
+            dma((strips,)),
+            dma((n_x, strips)),
+            dma((n_x, strips)),
+            dma((n_x, strips)),
+            dma((n_x, strips)),
+            dma((strips,)),
+            dma((strips,)),
         ],
         compiler_params=pltpu.CompilerParams(
             collective_id=0, has_side_effects=True, vmem_limit_bytes=56 * 2**20

time: 51.9 us -> 56.7 us (1.092)
  Pallas kernels: 48.6 us -> 54.5 us
  local copies, waits for them, and re-layouts: 2.44 us -> 1.36 us
    pallas_call x1, Pallas kernels: 48.6 us -> 54.5 us  [per_device(): pl.pallas_call(functools.partial(kernel, n_occ, n_vir, nb, n_o, lend), ou...]
    unnamed x4 -> x2, local copies, waits for them, and re-layouts: 2.44 us -> 1.36 us
where the time goes in v3:
time: 56.7 us; the launch traced here: 56.5 us
  Pallas kernels  54.5 us (96%)
  local copies, waits for them, and re-layouts  1.36 us (2%)
  between operations  0.64 us (1%)
    pallas_call x1, Pallas kernels, per_device(): pl.pallas_call(functools.partial(kernel, n_occ, n_vir, nb, n_o, lend), ou...  54.5 us
    unnamed x2, local copies, waits for them, and re-layouts  1.36 us

profile of v3, /device:TPU:0, one launch (start us, length us, event | category | flops | bytes accessed | tf_op | source)
XLA Modules:
  0.0 56.5 jit_solution(5235327677095625430)
XLA Ops:
  0.6 54.5 %shard_map.77 = (bf16[2,512,256]{2,1,0:T(8,128)(2,1)S(1)}, f32[2,8]{1,0:T(2,128)S(1)}) custom-call(bf16[2,512,256]{2,1,0:T(8,128)(2,1)} %bitcast.5, bf16[2,512,256]{2,1,0:T(8,128)(2,1)} %bitcast.6, bf16[2,8,8,8]{3,2,1,0:T(8,128)(2,1)} %w_ref.1, f32[8]{0:T(128)} %eo_ref.1, f32[1,256]{1,0:T(1,128)} %bitcast.7, s32[2,8]{1,0:T(2,128)} %mask_ref.1), custom_call_target="tpu_custom_call" | custom-call | flops 2147483648 | bytes 1572864 | tf_op jit(solution)/shard_map/pallas_call | solution.py:523
  55.1 0.8 %copy.10 = bf16[2,64,8,256]{3,2,1,0:T(8,128)(2,1)} copy(bf16[2,64,8,256]{3,2,1,0:T(8,128)(2,1)S(1)} %bitcast.4) | data formatting | bytes 1048576
  55.9 0.6 copy.11

commit v4 on v1

--- a/solution.py
+++ b/solution.py
@@ -25,9 +25,9 @@
 def kernel(
     n_occ, n_vir, nb, n_o,
     a_hbm, g_hbm, w_ref, eo_ref, ev_ref, mask_ref,
-    new_hbm, en_ref,
-    amps, panel, direct, wblk, acc, rden, newv, eall,
-    load_sem, z_send, z_recv, x_send, x_recv, c_send, c_recv, e_send, e_recv, out_sem,
+    new_ref, en_ref,
+    amps, panel, direct, wblk, acc, rden, eall,
+    load_sem, z_send, z_recv, x_send, x_recv, c_send, c_recv, e_send, e_recv,
 ):
     ri, rows, n_v = g_hbm.shape
     n_x = n_occ // 2
@@ -240,7 +240,7 @@
                 acc[i, rows_of(t), :] = value
                 return carry
             new = (value * rden[i, rows_of(t), :]).astype(BF16)
-            newv[i, rows_of(t), :] = new
+            new_ref[i, rows_of(t), :] = new
             prod = direct[i, rows_of(t), :].astype(F32) * new.astype(F32)
             return carry + jnp.sum(prod.reshape(TILE // n_o, n_o, n_v), axis=0)
 
@@ -248,8 +248,6 @@
             lax.fori_loop(0, tiles, body, 0)
             return
         energy = lax.fori_loop(0, tiles, body, jnp.zeros((n_o, n_v), F32))
-        out = pltpu.make_async_copy(newv.at[i], new_hbm.at[i], out_sem.at[i])
-        out.start()
         folded = energy[:, :LANES]
         for s in range(1, n_v // LANES):
             folded = folded + energy[:, s * LANES : (s + 1) * LANES]
@@ -313,7 +311,6 @@
     for i in range(ri):
         for d in range(1, n_vir):
             e_copy(d, i).wait_send()
-        pltpu.make_async_copy(newv.at[i], new_hbm.at[i], out_sem.at[i]).wait()
 
 
 def per_device(n_occ, n_vir, amps, integrals, ladder_ints, eps_occ, eps_vir, pair_mask):
@@ -326,8 +323,8 @@
     new, energy = pl.pallas_call(
         functools.partial(kernel, n_occ, n_vir, nb, n_o),
         out_shape=(
-            jax.ShapeDtypeStruct((ri, rows, n_v), BF16),
-            jax.ShapeDtypeStruct((ri, n_o), F32),
+            pltpu.VMEM((ri, rows, n_v), BF16),
+            pltpu.VMEM((ri, n_o), F32),
         ),
         in_specs=[
             pl.BlockSpec(memory_space=pl.ANY),
@@ -338,7 +335,7 @@
             pl.BlockSpec(memory_space=pltpu.SMEM),
         ],
         out_specs=(
-            pl.BlockSpec(memory_space=pl.ANY),
+            pl.BlockSpec(memory_space=pltpu.VMEM),
             pl.BlockSpec(memory_space=pltpu.VMEM),
         ),
         scratch_shapes=[
@@ -348,7 +345,6 @@
             pltpu.VMEM((ri, n_o, TILE, TILE), BF16),
             pltpu.VMEM((ri, rows, n_v), F32),
             pltpu.VMEM((ri, rows, n_v), F32),
-            pltpu.VMEM((ri, rows, n_v), BF16),
             pltpu.VMEM((n_vir, ri, n_o, LANES), F32),
             dma((ri + 1,)),
             dma((2, n_vir, n_chunks)),
@@ -359,7 +355,6 @@
             dma((n_x,)),
             dma((n_vir, ri)),
             dma((n_vir, ri)),
-            dma((ri,)),
         ],
         compiler_params=pltpu.CompilerParams(
             collective_id=0, has_side_effects=True, vmem_limit_bytes=56 * 2**20

time: 49.4 us -> 47.7 us (0.966)
  local copies, waits for them, and re-layouts: 2.44 us -> 1.36 us
  Pallas kernels: 46.1 us -> 45.5 us
    unnamed x4 -> x2, local copies, waits for them, and re-layouts: 2.44 us -> 1.36 us
    pallas_call x1, Pallas kernels: 46.1 us -> 45.5 us  [per_device(): pl.pallas_call(functools.partial(kernel, n_occ, n_vir, nb, n_o), out_shap...]
where the time goes in v4:
time: 47.7 us; the launch traced here: 47.5 us
  Pallas kernels  45.5 us (95%)
  local copies, waits for them, and re-layouts  1.36 us (3%)
  between operations  0.64 us (1%)
    pallas_call x1, Pallas kernels, per_device(): pl.pallas_call(functools.partial(kernel, n_occ, n_vir, nb, n_o), out_shap...  45.5 us
    unnamed x2, local copies, waits for them, and re-layouts  1.36 us

profile of v4, /device:TPU:0, one launch (start us, length us, event | category | flops | bytes accessed | tf_op | source)
XLA Modules:
  0.0 47.5 jit_solution(8876278640696441264)
XLA Ops:
  0.6 45.5 %shard_map.77 = (bf16[2,512,256]{2,1,0:T(8,128)(2,1)S(1)}, f32[2,8]{1,0:T(2,128)S(1)}) custom-call(bf16[2,512,256]{2,1,0:T(8,128)(2,1)} %bitcast.5, bf16[2,512,256]{2,1,0:T(8,128)(2,1)} %bitcast.6, bf16[2,8,8,8]{3,2,1,0:T(8,128)(2,1)} %w_ref.1, f32[8]{0:T(128)} %eo_ref.1, f32[1,256]{1,0:T(1,128)} %bitcast.7, s32[2,8]{1,0:T(2,128)} %mask_ref.1), custom_call_target="tpu_custom_call" | custom-call | flops 2147483648 | bytes 1572864 | tf_op jit(solution)/shard_map/pallas_call | solution.py:323
  46.2 0.8 %copy.10 = bf16[2,64,8,256]{3,2,1,0:T(8,128)(2,1)} copy(bf16[2,64,8,256]{3,2,1,0:T(8,128)(2,1)S(1)} %bitcast.4) | data formatting | bytes 1048576
  47.0 0.6 %copy.11 = f32[2,8]{1,0:T(2,128)} copy(f32[2,8]{1,0:T(2,128)S(1)} %get-tuple-element.7) | data formatting | bytes 128

commit v5 on v4

--- a/solution.py
+++ b/solution.py
@@ -11,7 +11,7 @@
 MESH = pl.DeviceIdType.MESH
 TILE = 256
 LANES = 128
-K_PARTS = 2
+K_PARTS = 4
 
 
 def iota(shape, axis):
@@ -33,6 +33,7 @@
     n_x = n_occ // 2
     tiles = rows // TILE
     k_per = n_o // K_PARTS
+    group = min(4, k_per)
     o_bits = n_o.bit_length() - 1
     chunks = [(i, h) for i in range(ri) for h in range(K_PARTS)]
 
@@ -229,13 +230,13 @@
         def body(t, carry):
             value = acc[i, rows_of(t), :]
 
-            def add(k4, value):
-                for kk in range(4):
-                    k = h * k_per + k4 * 4 + kk
+            def add(g, value):
+                for kk in range(group):
+                    k = h * k_per + g * group + kk
                     value = value + dot(amps[k, rows_of(t), :], panel[i, k])
                 return value
 
-            value = lax.fori_loop(0, k_per // 4, add, value)
+            value = lax.fori_loop(0, k_per // group, add, value)
             if not last:
                 acc[i, rows_of(t), :] = value
                 return carry

time: 47.7 us -> 48.2 us (1.010)
  Pallas kernels: 45.5 us -> 46 us
    pallas_call x1, Pallas kernels: 45.5 us -> 46 us  [per_device(): pl.pallas_call(functools.partial(kernel, n_occ, n_vir, nb, n_o), out_shap...]
where the time goes in v5:
time: 48.2 us; the launch traced here: 48 us
  Pallas kernels  46 us (95%)
  local copies, waits for them, and re-layouts  1.36 us (3%)
  between operations  0.64 us (1%)
    pallas_call x1, Pallas kernels, per_device(): pl.pallas_call(functools.partial(kernel, n_occ, n_vir, nb, n_o), out_shap...  46 us
    unnamed x2, local copies, waits for them, and re-layouts  1.36 us

profile of v5, /device:TPU:0, one launch (start us, length us, event | category | flops | bytes accessed | tf_op | source)
XLA Modules:
  0.0 48.0 jit_solution(14396392532528191774)
XLA Ops:
  0.6 46.0 %shard_map.77 = (bf16[2,512,256]{2,1,0:T(8,128)(2,1)S(1)}, f32[2,8]{1,0:T(2,128)S(1)}) custom-call(bf16[2,512,256]{2,1,0:T(8,128)(2,1)} %bitcast.5, bf16[2,512,256]{2,1,0:T(8,128)(2,1)} %bitcast.6, bf16[2,8,8,8]{3,2,1,0:T(8,128)(2,1)} %w_ref.1, f32[8]{0:T(128)} %eo_ref.1, f32[1,256]{1,0:T(1,128)} %bitcast.7, s32[2,8]{1,0:T(2,128)} %mask_ref.1), custom_call_target="tpu_custom_call" | custom-call | flops 2147483648 | bytes 1572864 | tf_op jit(solution)/shard_map/pallas_call | solution.py:324
  46.6 0.8 %copy.10 = bf16[2,64,8,256]{3,2,1,0:T(8,128)(2,1)} copy(bf16[2,64,8,256]{3,2,1,0:T(8,128)(2,1)S(1)} %bitcast.4) | data formatting | bytes 1048576
  47.4 0.6 %copy.11 = f32[2,8]{1,0:T(2,128)} copy(f32[2,8]{1,0:T(2,128)S(1)} %get-tuple-element.7) | data formatting | bytes 128
